TPU v7x, 256 devices: a whole 4x4x8 slice. The times are simulated.
256 devices in a mesh: inst: 32 (over y, z_hi, core), tp: 8 (over x, z_lo).
Axes of the slice: x: 4, y: 4, z: 8 (z_hi: 4, z_lo: 2; z = z_hi * 2 + z_lo), core: 2. Of those that a mesh axis runs over, the one named last changes fastest.
Arguments:
- queries: bfloat16 [3, 512, 8192], P(None, 'inst', 'tp'), may hold values from -18 to 18
- key_values: bfloat16 [512, 1024, 2048], P('inst', None, 'tp'), may hold values from -4 to 4
- new_key_values: bfloat16 [3, 512, 2048], P(None, 'inst', 'tp'), may hold values from -5 to 5
- cache_lengths: int32 [512], P('inst'), may hold values from 256 to 1021, as said below
- output_weight: bfloat16 [8192, 4096], P('tp'), may hold values from -0.0625 to 0.0625
- moving_requests: int32 [32, 4], P('inst'), may hold values from 0 to 15, as said below
- migration_plan: int32 [32, 4], replicated, may hold values from 0 to 31, as said below
- row_counts: int32 [3, 32, 4], replicated, may hold values from 1 to 32, as said below
- copied_rows: int32 [32, 4], P('inst'), may hold values from 0 to 160, as said below
- landing: bfloat16 [32, 4, 256, 2048], P('inst', None, None, 'tp'), may hold values from -6 to 6
Outputs:
- attended: bfloat16 [3, 512, 4096], P(None, 'inst', 'tp')
- landed: bfloat16 [32, 4, 256, 2048], P('inst', None, None, 'tp')
Inputs may be any that keep to these rules, and one draw needn't show every extreme that they name: `cache_lengths`: one resident request has exactly 1021 valid rows. `moving_requests`: an instance's 4 entries are distinct. For every lane m, migration_plan[., m] is a permutation of the instances; an instance's destinations are distinct and never the instance itself. `row_counts`: some count equals 32. `copied_rows`: some slot holds exactly 160 rows.
All inputs are finite; a program needn't handle non-finite values.
Results may differ from a plain program's by a relative error of at most 0.0057.
Values may be sent and summed in bfloat16 or wider, within the bound.
A program may use at most 128 MiB of HBM per device.

v0:
```python
import math

import jax
import jax.numpy as jnp
from jax import lax
from jax.sharding import PartitionSpec as P

HEAD_DIM = 128
STEPS = 3
MOST_ROWS = 32


def attend(query, key_values, new_key_values, cache_lengths, first_step):
    spans, requests, query_width = query.shape
    length = key_values.shape[1]
    kv_local = key_values.shape[2] // (2 * HEAD_DIM)
    group_size = query_width // (kv_local * HEAD_DIM)
    factor = 1.0 / math.sqrt(HEAD_DIM)
    query_heads = query.reshape(spans, requests, kv_local, group_size, HEAD_DIM)
    stored = key_values.reshape(requests, length, kv_local, 2, HEAD_DIM)
    newest = new_key_values.reshape(STEPS, requests, kv_local, 2, HEAD_DIM)
    old_scores = (
        jnp.einsum(
            "sbkgd,blkd->sbkgl", query_heads, stored[:, :, :, 0], preferred_element_type=jnp.float32
        )
        * factor
    )
    new_scores = (
        jnp.einsum(
            "sbkgd,tbkd->sbkgt", query_heads, newest[:, :, :, 0], preferred_element_type=jnp.float32
        )
        * factor
    )
    old_mask = (jnp.arange(length, dtype=jnp.int32)[None, :] < cache_lengths[:, None])[
        None, :, None, None, :
    ]
    step_ids = jnp.arange(STEPS, dtype=jnp.int32)
    new_mask = (step_ids[None, :] <= first_step + jnp.arange(spans, dtype=jnp.int32)[:, None])[
        :, None, None, None, :
    ]
    highest = jnp.maximum(
        jnp.max(jnp.where(old_mask, old_scores, -jnp.inf), axis=-1),
        jnp.max(jnp.where(new_mask, new_scores, -jnp.inf), axis=-1),
    )
    old_exp = jnp.where(old_mask, jnp.exp(old_scores - highest[..., None]), 0.0)
    new_exp = jnp.where(new_mask, jnp.exp(new_scores - highest[..., None]), 0.0)
    denominator = jnp.sum(old_exp, axis=-1) + jnp.sum(new_exp, axis=-1)
    old_weight = (old_exp / denominator[..., None]).astype(jnp.bfloat16)
    new_weight = (new_exp / denominator[..., None]).astype(jnp.bfloat16)
    context = jnp.einsum(
        "sbkgl,blkd->sbkgd", old_weight, stored[:, :, :, 1], preferred_element_type=jnp.float32
    )
    context = context + jnp.einsum(
        "sbkgt,tbkd->sbkgd", new_weight, newest[:, :, :, 1], preferred_element_type=jnp.float32
    )
    return context.reshape(spans, requests, query_width).astype(jnp.bfloat16)


def tail_rows(key_values, cache_lengths, chosen, own_counts):
    overall = jnp.sum(own_counts, axis=0)
    offsets = jnp.cumsum(own_counts, axis=0) - own_counts
    starts = cache_lengths[chosen][None, :] - overall[None, :] + offsets
    span = jnp.arange(MOST_ROWS, dtype=jnp.int32)
    positions = jnp.clip(starts.T[:, :, None] + span, 0, key_values.shape[1] - 1)
    return key_values[chosen[:, None, None], positions]


def place_rows(slots, copied, incoming_counts, arrived, current):
    moving, most_rows = (arrived.shape[0], arrived.shape[1])
    offsets = jnp.sum(incoming_counts[:current], axis=0)
    span = jnp.arange(most_rows, dtype=jnp.int32)
    position = copied[:, None] + offsets[:, None] + span[None, :]
    position = jnp.where(
        span[None, :] < incoming_counts[current][:, None], position, slots.shape[1]
    )
    lane_ids = jnp.arange(moving, dtype=jnp.int32)[:, None]
    return slots.at[lane_ids, position].set(arrived, mode="drop")


def on_device(
    queries,
    key_values,
    new_key_values,
    cache_lengths,
    output_weight,
    moving_requests,
    migration_plan,
    row_counts,
    copied_rows,
    landing,
):
    context = jnp.concatenate(
        [
            attend(
                queries[current : current + 1], key_values, new_key_values, cache_lengths, current
            )
            for current in range(STEPS)
        ],
        axis=0,
    )
    partial_sums = jnp.einsum(
        "sbq,qo->sbo", context, output_weight, preferred_element_type=jnp.float32
    )
    attended = lax.psum_scatter(partial_sums, "tp", scatter_dimension=2, tiled=True).astype(
        jnp.bfloat16
    )
    instances = lax.axis_size("inst")
    own_index = lax.axis_index("inst")
    lane_ids = jnp.arange(migration_plan.shape[1], dtype=jnp.int32)
    matches = migration_plan == own_index
    senders = jnp.sum(
        jnp.where(matches, jnp.arange(instances, dtype=jnp.int32)[:, None], 0), axis=0
    )
    outgoing = tail_rows(key_values, cache_lengths, moving_requests[0], row_counts[:, own_index, :])
    incoming_counts = row_counts[:, senders, lane_ids]
    slots = landing[0]
    copied = copied_rows[0]
    for current in range(STEPS):
        pieces = outgoing[:, current]
        everyone = lax.all_gather(pieces[None], "inst", axis=0, tiled=True)
        slots = place_rows(slots, copied, incoming_counts, everyone[senders, lane_ids], current)
    return (attended, slots[None])


def solution(mesh):
    placed = (
        P(None, "inst", "tp"),
        P("inst", None, "tp"),
        P(None, "inst", "tp"),
        P("inst"),
        P("tp", None),
        P("inst", None),
        P(),
        P(),
        P("inst", None),
        P("inst", None, None, "tp"),
    )
    return jax.shard_map(
        on_device,
        mesh=mesh,
        in_specs=placed,
        out_specs=(P(None, "inst", "tp"), P("inst", None, None, "tp")),
        check_vma=False,
    )
```

profile of v0, /device:TPU:1, one launch (start us, length us, event | category | flops | bytes accessed | tf_op | source)
XLA Modules:
  0.0 260.7 jit_solution(5214255339663308089)
XLA Ops:
  8.1 12.3 %copy.21 = bf16[16,1024,256]{1,2,0:T(8,128)(2,1)} copy(bf16[16,1024,256]{2,1,0:T(8,128)(2,1)} %param.11) | data formatting | bytes 16777216 | tf_op args[1]
  20.5 2.9 %fusion.11 = f32[16,1,1024,1,8]{2,4,0,3,1:T(8,128)S(1)} fusion(bf16[16,8,128]{2,1,0:T(8,128)(2,1)S(1)} %bitcast.227, bf16[16,1024,1,2,128]{1,4,3,0,2:T(8,128)(2,1)} %bitcast.211), kind=kOutput, calls=%fused_computation.22 | convolution fusion | flops 33685504 | bytes 4751360 | tf_op jit(solution)/shard_map/sbkgd,blkd->sbkgl/dot_general | solution.py:23
  23.3 2.8 %fusion.13 = f32[16,1,1024,1,8]{2,4,0,3,1:T(8,128)S(1)} fusion(bf16[16,8,128]{2,1,0:T(8,128)(2,1)S(1)} %bitcast.229, bf16[16,1024,1,2,128]{1,4,3,0,2:T(8,128)(2,1)} %bitcast.212), kind=kOutput, calls=%fused_computation.24 | convolution fusion | flops 33685504 | bytes 4751360 | tf_op jit(solution)/shard_map/sbkgd,blkd->sbkgl/dot_general | solution.py:23
  26.2 0.1 iota_compare_fusion
  26.3 0.2 select_reduce_fusion.3
  26.5 0.2 select_reduce_fusion.4
  26.7 0.2 select_reduce_fusion.5
  26.8 3.1 %select_reduce_fusion.2 = (f32[16,8]{1,0:T(8,128)S(1)}, f32[16,8]{1,0:T(8,128)S(1)}, f32[16,8]{1,0:T(8,128)S(1)}, f32[16,1,1024,1,8]{2,4,0,3,1:T(8,128)S(1)}) fusion(pred[16,1024]{1,0:T(8,128)(4,1)S(1)} %iota_compare_fusion, f32[16,1,1024,1,8]{2,4,0,3,1:T(8,128)S(1)} %fusion.11, f32[16,1,1024,1,8]{2,4,0,3,1:T(8,128)S(1)} %fusion.13, ...), kind=kOutput, calls=%fused_computation.54 | convolution fusion | flops 34471552 | bytes 5817856 | tf_op jit(solution)/shard_map/sbkgd,blkd->sbkgl/dot_general | solution.py:23
  29.9 0.1 bitcast_reduce_fusion.5
  30.0 0.5 bitcast_reduce_fusion.2
  30.6 3.4 %fusion.7 = f32[16,8,128]{2,1,0:T(8,128)S(1)} fusion(bf16[16,1024,1,2,128]{1,4,3,0,2:T(8,128)(2,1)} %bitcast.214, f32[16,1,1024,1,8]{2,4,0,3,1:T(8,128)S(1)} %get-tuple-element.23, f32[16,8]{1,0:T(8,128)S(1)} %add.230, f32[16,8]{1,0:T(8,128)S(1)} %max.33, pred[16,1024]{1,0:T(8,128)(4,1)S(1)} %iota_compare_fusion), kind=kOutput, calls=%fused_computation.18 | convolution fusion | flops 34078720 | bytes 4801536 | tf_op jit(solution)/shard_map/sbkgl,blkd->sbkgd/dot_general | solution.py:50
  34.0 0.3 fusion.19
  34.3 0.1 bitcast_reduce_fusion.4
  34.4 3.4 %fusion.6 = f32[16,8,128]{2,1,0:T(8,128)S(1)} fusion(bf16[16,1024,1,2,128]{1,4,3,0,2:T(8,128)(2,1)} %bitcast.215, f32[16,1,1024,1,8]{2,4,0,3,1:T(8,128)S(1)} %fusion.11, f32[16,8]{1,0:T(8,128)S(1)} %add.232, f32[16,8]{1,0:T(8,128)S(1)} %max.34, pred[16,1024]{1,0:T(8,128)(4,1)S(1)} %iota_compare_fusion), kind=kOutput, calls=%fused_computation.17 | convolution fusion | flops 34078720 | bytes 4801536 | tf_op jit(solution)/shard_map/sbkgl,blkd->sbkgd/dot_general | solution.py:50
  37.8 0.3 fusion.18
  38.2 0.1 bitcast_reduce_fusion.3
  38.3 3.4 %fusion.5 = f32[16,8,128]{2,1,0:T(8,128)S(1)} fusion(bf16[16,1024,1,2,128]{1,4,3,0,2:T(8,128)(2,1)} %bitcast.216, f32[16,1,1024,1,8]{2,4,0,3,1:T(8,128)S(1)} %fusion.13, f32[16,8]{1,0:T(8,128)S(1)} %add.234, f32[16,8]{1,0:T(8,128)S(1)} %max.35, pred[16,1024]{1,0:T(8,128)(4,1)S(1)} %iota_compare_fusion), kind=kOutput, calls=%fused_computation.16 | convolution fusion | flops 34078720 | bytes 4801536 | tf_op jit(solution)/shard_map/sbkgl,blkd->sbkgd/dot_general | solution.py:50
  41.7 0.3 fusion.17
  42.1 5.8 %fusion = f32[3,16,4096]{2,1,0:T(8,128)} fusion(bf16[1024,4096]{1,0:T(8,128)(2,1)} %param.14, bf16[1,16,1024]{2,1,0:T(8,128)(2,1)S(1)} %convert_element_type.110, bf16[1,16,1024]{2,1,0:T(8,128)(2,1)S(1)} %convert_element_type.103, bf16[1,16,1024]{2,1,0:T(8,128)(2,1)S(1)} %convert_element_type.96), kind=kOutput, calls=%fused_computation.9 | convolution fusion | flops 402751488 | bytes 9273344 | tf_op jit(solution)/shard_map/sbq,qo->sbo/dot_general | solution.py:101
  48.0 0.2 dynamic-slice_reduce_fusion.1
  48.3 0.6 gather_fusion.1
  48.9 0.1 copy.27
  49.1 0.1 reshape.670
  49.2 9.2 %gather_fusion.2 = bf16[384,256]{1,0:T(8,128)(2,1)S(1)} fusion(bf16[16,1024,256]{2,1,0:T(8,128)(2,1)} %param.11, s32[384]{0:T(512)S(1)} %reshape.670), kind=kCustom, calls=%fused_computation.2 | custom fusion | bytes 396288 | tf_op jit(solution)/shard_map/gather | solution.py:65
  58.4 0.7 fusion.91
  59.2 0.5 all-gather.9.cloned.1.call-update
  59.7 0.2 all-gather.11.cloned.1.call-start
  59.9 0.3 all-gather.11.cloned.1.call-update
  60.3 0.1 copy.26
  60.4 0.1 select_reduce_fusion.6
  60.5 0.6 gather_fusion
  61.1 0.2 slice_reduce_fusion.1
  61.4 0.1 reshape.694
  61.5 0.1 slice_reduce_fusion
  61.7 0.1 reshape.700
  61.9 0.1 reshape.706
  62.0 27.6 %reduce-scatter.2.cloned.1.call-done = f32[3,16,512]{2,1,0:T(8,128)} async-done(((f32[3,16,4096]{2,1,0:T(8,128)}), f32[3,16,512]{2,1,0:T(8,128)}) %reduce-scatter.2.cloned.1.call-update) | async-done | bytes 98320 | tf_op jit(solution)/shard_map/reduce_scatter | solution.py:104
  89.6 1.5 convert_element_type.111
  91.1 27.4 %all-gather.7.cloned.1.call-done = bf16[128,1,32,256]{3,2,1,0:T(8,128)(2,1)} async-done(((bf16[4,1,32,256]{3,2,1,0:T(8,128)(2,1)}), bf16[128,1,32,256]{3,2,1,0:T(8,128)(2,1)}) %all-gather.7.cloned.1.call-update) | async-done | bytes 2097168 | tf_op jit(solution)/shard_map/all_gather | solution.py:120
  118.5 2.1 gather_fusion.3
  120.6 52.3 %all-gather.9.cloned.1.call-done = bf16[128,1,32,256]{3,2,1,0:T(8,128)(2,1)} async-done(((bf16[4,1,32,256]{3,2,1,0:T(8,128)(2,1)}), bf16[128,1,32,256]{3,2,1,0:T(8,128)(2,1)}) %all-gather.9.cloned.1.call-update) | async-done | bytes 2097168 | tf_op jit(solution)/shard_map/all_gather | solution.py:120
  172.9 2.1 gather_fusion.4
  175.1 52.9 %all-gather.11.cloned.1.call-done = bf16[128,1,32,256]{3,2,1,0:T(8,128)(2,1)} async-done(((bf16[4,1,32,256]{3,2,1,0:T(8,128)(2,1)}), bf16[128,1,32,256]{3,2,1,0:T(8,128)(2,1)}) %all-gather.11.cloned.1.call-update) | async-done | bytes 2097168 | tf_op jit(solution)/shard_map/all_gather | solution.py:120
  227.9 2.1 gather_fusion.5
  230.1 7.4 %scatter_fusion = bf16[4,256,256]{2,1,0:T(8,128)(2,1)S(1)} fusion(bf16[4,256,256]{2,1,0:T(8,128)(2,1)S(1)} %bitcast.218, s32[128]{0:T(128)S(1)} %reshape.694, bf16[128,256]{1,0:T(8,128)(2,1)S(1)} %bitcast.220), kind=kCustom, calls=%fused_computation.6 | custom fusion | bytes 197632 | tf_op jit(solution)/shard_map/scatter | solution.py:77
  237.5 7.4 %scatter_fusion.1 = bf16[4,256,256]{2,1,0:T(8,128)(2,1)S(1)} fusion(bf16[4,256,256]{2,1,0:T(8,128)(2,1)S(1)} %scatter_fusion, s32[128]{0:T(128)S(1)} %reshape.700, bf16[128,256]{1,0:T(8,128)(2,1)S(1)} %bitcast.221), kind=kCustom, calls=%fused_computation.7 | custom fusion | bytes 197632 | tf_op jit(solution)/shard_map/scatter | solution.py:77
  244.9 7.4 %scatter_fusion.2 = bf16[4,256,256]{2,1,0:T(8,128)(2,1)S(1)} fusion(bf16[4,256,256]{2,1,0:T(8,128)(2,1)S(1)} %scatter_fusion.1, s32[128]{0:T(128)S(1)} %reshape.706, bf16[128,256]{1,0:T(8,128)(2,1)S(1)} %bitcast.222), kind=kCustom, calls=%fused_computation.8 | custom fusion | bytes 197632 | tf_op jit(solution)/shard_map/scatter | solution.py:77
  252.3 0.8 copy-done.1
  (52 shorter events, 0.8 us)
Async XLA Ops:
  8.0 81.6 %reduce-scatter.2.cloned.1.call-start = ((), (), s32[]{:S(2)}) async-start(), calls=%async_computation.1 | async-start | bytes 884736 | tf_op jit(solution)/shard_map/reduce_scatter | solution.py:104
  8.1 12.3 %copy-start.3 = (bf16[3,16,1024]{2,1,0:T(8,128)(2,1)S(1)}, bf16[3,16,1024]{2,1,0:T(8,128)(2,1)}, u32[]{:S(2)}) copy-start(bf16[3,16,1024]{2,1,0:T(8,128)(2,1)} %param.10) | copy-start | bytes 294916
  20.4 5.8 %copy-start = (s32[16]{0:T(128)S(1)}, s32[16]{0:T(128)}, u32[]{:S(2)}) copy-start(s32[16]{0:T(128)} %param.13) | copy-start | bytes 196
  20.4 5.9 %copy-start.4 = (bf16[3,16,256]{2,1,0:T(8,128)(2,1)S(1)}, bf16[3,16,256]{2,1,0:T(8,128)(2,1)}, u32[]{:S(2)}) copy-start(bf16[3,16,256]{2,1,0:T(8,128)(2,1)} %param.12) | copy-start | bytes 73732
  38.3 9.7 %copy-start.5 = (s32[3,32,4]{1,2,0:T(4,128)S(1)}, s32[3,32,4]{1,2,0:T(4,128)}, u32[]{:S(2)}) copy-start(s32[3,32,4]{1,2,0:T(4,128)} %param.17) | copy-start | bytes 4612
  38.3 10.0 %copy-start.8 = (s32[1,4]{1,0:T(1,128)S(1)}, s32[1,4]{1,0:T(1,128)}, u32[]{:S(2)}) copy-start(s32[1,4]{1,0:T(1,128)} %param.15) | copy-start | bytes 52
  41.7 18.7 %copy-start.6 = (s32[32,4]{0,1:T(4,128)S(1)}, s32[32,4]{0,1:T(4,128)}, u32[]{:S(2)}) copy-start(s32[32,4]{0,1:T(4,128)} %param.16) | copy-start | bytes 1540
  41.7 19.6 %copy-start.7 = (s32[1,4]{1,0:T(1,128)S(1)}, s32[1,4]{1,0:T(1,128)}, u32[]{:S(2)}) copy-start(s32[1,4]{1,0:T(1,128)} %param.18) | copy-start | bytes 52
  41.7 188.4 %copy-start.2 = (bf16[1,4,256,256]{3,2,1,0:T(8,128)(2,1)S(1)}, bf16[1,4,256,256]{3,2,1,0:T(8,128)(2,1)}, u32[]{:S(2)}) copy-start(bf16[1,4,256,256]{3,2,1,0:T(8,128)(2,1)} %param.19) | copy-start | bytes 1572868
  47.9 70.6 %all-gather.7.cloned.1.call-start = ((), (), s32[]{:S(2)}) async-start(), calls=%async_computation.2 | async-start | bytes 2162688 | tf_op jit(solution)/shard_map/all_gather | solution.py:120
  59.1 113.8 %all-gather.9.cloned.1.call-start = ((), (), s32[]{:S(2)}) async-start(), calls=%async_computation.3 | async-start | bytes 2162688 | tf_op jit(solution)/shard_map/all_gather | solution.py:120
  59.7 168.2 %all-gather.11.cloned.1.call-start = ((), (), s32[]{:S(2)}) async-start(), calls=%async_computation.4 | async-start | bytes 2162688 | tf_op jit(solution)/shard_map/all_gather | solution.py:120
  252.3 0.8 copy-start.1
Sparse Core Ops, SparseCore 0:
  48.1 41.5 reduce-scatter.1
Sparse Core Ops, SparseCore 1:
  59.2 59.2 all-gather.6
  121.2 51.6 all-gather.8
  176.3 51.6 all-gather.10
where the time goes:
time: 261 us
  waiting for transfers between devices  161 us (62%)
  local copies, waits for them, and re-layouts  53.7 us (21%)
  matrix products  26.2 us (10%)
  between operations  16 us (6%)
  other arithmetic  3.31 us (1%)
    all_gather x3, waiting for transfers between devices, on_device(): everyone = lax.all_gather(pieces[None], 'inst', axis=0, tiled=True)  133 us
    reduce_scatter x1, waiting for transfers between devices, on_device(): lax.psum_scatter(partial_sums, 'tp', scatter_dimension=2, tiled=True)  27.6 us
    scatter x3, local copies, waits for them, and re-layouts, place_rows(): return slots.at[lane_ids, position].set(arrived, mode='drop')  22.1 us
    unnamed x24, local copies, waits for them, and re-layouts  13.3 us
    dot_general x3, matrix products, attend(): jnp.einsum('sbkgl,blkd->sbkgd', old_weight, stored[:, :, :, 1], preferred...  10.3 us
    gather x1, local copies, waits for them, and re-layouts, tail_rows(): return key_values[chosen[:, None, None], positions]  9.22 us
    dot_general x3, matrix products, attend(): jnp.einsum('sbkgd,blkd->sbkgl', query_heads, stored[:, :, :, 0], preferre...  8.76 us
    gather x3, local copies, waits for them, and re-layouts, on_device(): everyone[senders, lane_ids]  6.43 us
  transfers between devices with their start and end apart: 4, of which 4 were waited for; matrix products, arithmetic and copies ran while one was open for 7% of the time, Pallas kernels for 0%

commit v1 on v0

v1 whole, which is shorter than its diff:
```python
import functools
import math

import jax
import jax.numpy as jnp
from jax import lax
from jax.experimental import pallas as pl
from jax.experimental.pallas import tpu as pltpu
from jax.sharding import PartitionSpec as P

HEAD_DIM = 128
STEPS = 3
HEADS = 8
REQS = 16
CACHE = 1024
MOVING = 4
MOST_ROWS = 32
LANE_ROWS = STEPS * MOST_ROWS
LAND_ROWS = 256
INSTS = 32
CHIPS = 16
TP = 8
OUT_WIDTH = 4096
ROWS = STEPS * HEADS
TOKENS = STEPS * REQS
WIDE = OUT_WIDTH // 4
NARROW = OUT_WIDTH // TP
GROUP = 4
GROUPS = REQS // GROUP
TILE = 16
TILES = CACHE // TILE
WINDOW = LANE_ROWS + TILE
LOW = -1e30
SCALE = math.log2(math.e) / math.sqrt(HEAD_DIM)
F32 = jnp.float32
BF16 = jnp.bfloat16
I32 = jnp.int32


def iota(shape, dim):
    return lax.broadcasted_iota(I32, shape, dim)


def wait_bytes(ref, sem):
    pltpu.make_async_copy(ref, ref, sem).wait()


def main_kernel(
    lengths_hbm,
    moving_hbm,
    copied_hbm,
    queries_hbm,
    newest_hbm,
    cache_hbm,
    weight_hbm,
    plan_hbm,
    counts_hbm,
    landing_hbm,
    attended,
    landed,
    lengths,
    moving,
    copied,
    queries,
    newest,
    cache,
    weight,
    plan,
    counts,
    landing,
    meta_vec,
    meta,
    ordered,
    regroup,
    new_scores,
    acc,
    top,
    norm,
    scatter_out,
    scatter_in,
    forward_out,
    forward_in,
    wide_out,
    wide_in,
    wide_own,
    narrow_out,
    narrow_in,
    small_sem,
    cache_sem,
    weight_sem,
    landing_sem,
    meta_sem,
    scatter_sem,
    forward_sem,
    wide_send_sem,
    wide_recv_sem,
    narrow_sem,
):
    me = lax.axis_index("inst")
    tp = lax.axis_index("tp")
    chip = me // 2
    core = lax.rem(me, 2)
    column = tp // 2
    side = lax.rem(tp, 2)
    lane = chip // 4

    barrier = pltpu.get_barrier_semaphore()

    def greet(o, carry):
        pl.semaphore_signal(
            barrier, inc=1, device_id={"inst": lax.rem(me + o, INSTS)}
        )
        return carry

    small = [
        pltpu.make_async_copy(src, dst, small_sem.at[n])
        for n, (src, dst) in enumerate(
            [
                (queries_hbm, queries),
                (newest_hbm, newest),
                (plan_hbm, plan),
                (counts_hbm, counts),
                (lengths_hbm, lengths),
                (moving_hbm, moving),
                (copied_hbm, copied),
            ]
        )
    ]
    for copy in small:
        copy.start()
    cache_loads = []
    for g in range(GROUPS):
        part = pl.ds(g * GROUP * TILES, GROUP * TILES)
        cache_loads.append(
            pltpu.make_async_copy(cache_hbm.at[part], cache.at[part], cache_sem.at[g])
        )
        cache_loads[-1].start()
    lax.fori_loop(1, INSTS, greet, 0)
    for k in range(3):
        other = lax.rem(column + 1 + k, 4)
        pl.semaphore_signal(barrier, inc=1, device_id={"tp": other * 2 + side})
    pl.semaphore_signal(barrier, inc=1, device_id={"tp": column * 2 + 1 - side})
    weight_loads = []
    for k in range(4):
        target = lax.rem(column + 1 + k, 4)
        weight_loads.append(
            pltpu.make_async_copy(
                weight_hbm.at[:, pl.ds(pl.multiple_of(target * WIDE, WIDE), WIDE)],
                weight.at[k],
                weight_sem.at[k],
            )
        )
        weight_loads[-1].start()
    landing_load = pltpu.make_async_copy(landing_hbm, landing, landing_sem.at[0])
    landing_load.start()

    for copy in small:
        copy.wait()
    inst_rows = iota((INSTS, INSTS), 0)
    inst_cols = iota((INSTS, INSTS), 1)
    total = counts[0] + counts[1] + counts[2]
    for m in range(MOVING):
        hit = plan[m : m + 1, :] == inst_rows
        sender = jnp.sum(jnp.where(hit, inst_cols, 0), axis=1, keepdims=True)
        meta_vec[0:INSTS, m : m + 1] = jnp.minimum(sender, INSTS - 1)
        meta_vec[0:INSTS, MOVING + m : MOVING + m + 1] = jnp.sum(
            jnp.where(hit, total[m : m + 1, :], 0), axis=1, keepdims=True
        )
    meta_vec[INSTS : INSTS + MOVING, 0:INSTS] = total
    meta_load = pltpu.make_async_copy(meta_vec, meta, meta_sem.at[0])
    meta_load.start()

    stacked = jnp.concatenate(
        [
            queries[s, :, h * HEAD_DIM : (h + 1) * HEAD_DIM]
            for s in range(STEPS)
            for h in range(HEADS)
        ],
        axis=0,
    )
    pick = iota((ROWS, REQS * ROWS), 1) - REQS * iota((ROWS, REQS * ROWS), 0)
    order = jnp.concatenate(
        [(pick == b).astype(F32) for b in range(REQS)], axis=0
    ).astype(BF16)
    ordered[...] = jnp.dot(order, stacked, preferred_element_type=F32)
    back = iota((REQS, REQS * ROWS), 1) - ROWS * iota((REQS, REQS * ROWS), 0)
    for h in range(HEADS):
        for s in range(STEPS):
            n = (h * STEPS + s) * REQS
            regroup[n : n + REQS, :] = (back == s * HEADS + h).astype(F32).astype(BF16)
    fresh = lax.dot_general(
        ordered[...].astype(BF16),
        newest[:, :HEAD_DIM],
        (((1,), (1,)), ((), ())),
        preferred_element_type=F32,
    )
    position = iota((ROWS, TOKENS), 1)
    causal = (position >> 4) <= (iota((ROWS, TOKENS), 0) >> 3)
    for b in range(REQS):
        rows = slice(b * ROWS, (b + 1) * ROWS)
        valid = causal & ((position & (REQS - 1)) == b)
        new_scores[rows, :] = jnp.where(valid, fresh[rows] * SCALE, LOW)

    def attend_group(g):
        members = range(g * GROUP, (g + 1) * GROUP)
        rows = [slice(b * ROWS, (b + 1) * ROWS) for b in members]
        stored = [
            cache[b * TILES : (b + 1) * TILES].reshape(CACHE, 2 * HEAD_DIM) for b in members
        ]
        scores = [
            lax.dot_general(
                ordered[r, :].astype(BF16),
                kv[:, :HEAD_DIM],
                (((1,), (1,)), ((), ())),
                preferred_element_type=F32,
            )
            for r, kv in zip(rows, stored)
        ]
        scores = [
            jnp.where(iota((ROWS, CACHE), 1) < lengths[b], x * SCALE, LOW)
            for b, x in zip(members, scores)
        ]
        highest = [
            jnp.maximum(
                jnp.max(x, axis=1, keepdims=True),
                jnp.max(new_scores[r, :], axis=1, keepdims=True),
            )
            for r, x in zip(rows, scores)
        ]
        weights = [jnp.exp2(x - h) for x, h in zip(scores, highest)]
        sums = [jnp.sum(w, axis=1, keepdims=True) for w in weights]
        outs = [
            jnp.dot(w.astype(BF16), kv[:, HEAD_DIM:], preferred_element_type=F32)
            for w, kv in zip(weights, stored)
        ]
        for r, h, n, o in zip(rows, highest, sums, outs):
            top[r, :] = jnp.broadcast_to(h, (ROWS, HEAD_DIM))
            norm[r, :] = jnp.broadcast_to(n, (ROWS, HEAD_DIM))
            acc[r, :] = o

    for g in range(GROUPS - 1):
        cache_loads[g].wait()
        attend_group(g)
    cache_loads[GROUPS - 1].wait()

    meta_load.wait()
    tail_rows = iota((LANE_ROWS, WINDOW), 0)
    tail_cols = iota((LANE_ROWS, WINDOW), 1)
    for m in range(MOVING):
        request = moving[0, m]
        total = meta[INSTS + m, me]
        start = lengths[request] - total
        first = jnp.minimum(start // TILE, TILES - WINDOW // TILE)
        window = jnp.concatenate(
            [cache[request * TILES + first + t] for t in range(WINDOW // TILE)], axis=0
        )
        shift = (tail_cols - tail_rows == start - first * TILE) & (tail_rows < total)
        tail = jnp.dot(
            shift.astype(F32).astype(BF16), window, preferred_element_type=F32
        ).astype(BF16)
        for q in range(12):
            r, c = (q // 2) * 16, (q % 2) * 128
            scatter_out[m * 12 + q] = tail[r : r + 16, c : c + 128]

    pl.semaphore_wait(barrier, INSTS - 1 + 3 + 1)

    def scatter_two(target_chip, sem):
        return pltpu.make_async_remote_copy(
            src_ref=scatter_out.at[pl.ds(target_chip * 3, 2)],
            dst_ref=scatter_in.at[me],
            send_sem=sem,
            recv_sem=scatter_sem.at[0],
            device_id={"inst": target_chip * 2},
        )

    def scatter_one(target_chip, sem):
        return pltpu.make_async_remote_copy(
            src_ref=scatter_out.at[pl.ds(target_chip * 3 + 2, 1)],
            dst_ref=scatter_in.at[me, pl.ds(0, 1)],
            send_sem=sem,
            recv_sem=scatter_sem.at[0],
            device_id={"inst": target_chip * 2 + 1},
        )

    def scatter(o, carry):
        target_chip = lax.rem(chip + o, CHIPS)
        scatter_two(target_chip, scatter_sem.at[1]).start()
        scatter_one(target_chip, scatter_sem.at[1]).start()
        return carry

    lax.fori_loop(1, CHIPS, scatter, 0)

    @pl.when(core == 0)
    def _():
        scatter_one(chip, scatter_sem.at[2]).start()
        scatter_in[me] = scatter_out[pl.ds(chip * 3, 2)]

    @pl.when(core == 1)
    def _():
        scatter_two(chip, scatter_sem.at[2]).start()
        scatter_in[me, 0] = scatter_out[chip * 3 + 2]

    attend_group(GROUPS - 1)

    late = jnp.exp2(new_scores[...] - top[:, :TOKENS])
    whole = norm[...] + jnp.sum(late, axis=1, keepdims=True)
    context = acc[...] + jnp.dot(
        late.astype(BF16), newest[:, HEAD_DIM:], preferred_element_type=F32
    )
    context = (context / whole).astype(BF16)
    context = jnp.dot(regroup[...], context, preferred_element_type=F32).astype(BF16)
    context = jnp.concatenate(
        [context[h * TOKENS : (h + 1) * TOKENS] for h in range(HEADS)], axis=1
    )

    wide_sends = []

    def project(k):
        weight_loads[k].wait()
        partial = jnp.dot(context, weight[k], preferred_element_type=F32)
        if k < 3:
            wide_out[k] = partial.astype(BF16)
            copy = pltpu.make_async_remote_copy(
                src_ref=wide_out.at[k],
                dst_ref=wide_in.at[k],
                send_sem=wide_send_sem.at[k],
                recv_sem=wide_recv_sem.at[k],
                device_id={"tp": lax.rem(column + 1 + k, 4) * 2 + side},
            )
            copy.start()
            wide_sends.append(copy)
        else:
            wide_own[...] = partial

    for k in range(4):
        project(k)

    def forward_two(target):
        return pltpu.make_async_remote_copy(
            src_ref=forward_out.at[target],
            dst_ref=forward_in.at[pl.ds(chip * 3, 2)],
            send_sem=forward_sem.at[1],
            recv_sem=forward_sem.at[0],
            device_id={"inst": target},
        )

    def forward_one(target):
        return pltpu.make_async_remote_copy(
            src_ref=forward_out.at[target, pl.ds(0, 1)],
            dst_ref=forward_in.at[pl.ds(chip * 3 + 2, 1)],
            send_sem=forward_sem.at[1],
            recv_sem=forward_sem.at[0],
            device_id={"inst": target},
        )

    @pl.when(core == 0)
    def _():
        wait_bytes(scatter_in.at[pl.ds(0, INSTS - 1)], scatter_sem.at[0])

        for d in range(INSTS):
            forward_out[d] = scatter_in[meta[d, lane]]

        def forward(o, carry):
            forward_two(lax.rem(me + o, INSTS)).start()
            return carry

        lax.fori_loop(1, INSTS, forward, 0)
        forward_in[pl.ds(chip * 3, 2)] = scatter_in[meta[me, lane]]

    @pl.when(core == 1)
    def _():
        wait_bytes(scatter_in.at[pl.ds(0, INSTS - 1), 0], scatter_sem.at[0])

        for d in range(INSTS):
            forward_out[d, 0] = scatter_in[meta[d, lane], 0]

        def forward(o, carry):
            forward_one(lax.rem(me + o, INSTS)).start()
            return carry

        lax.fori_loop(1, INSTS, forward, 0)
        forward_in[chip * 3 + 2] = scatter_in[meta[me, lane], 0]

    for k in range(3):
        pltpu.make_async_copy(wide_in.at[k], wide_in.at[k], wide_recv_sem.at[k]).wait()
    total = wide_own[...]
    for k in range(3):
        total = total + wide_in[k].astype(F32)
    left, right = total[:, :NARROW], total[:, NARROW:]
    narrow_out[...] = jnp.where(side == 0, right, left).astype(BF16)
    narrow_send = pltpu.make_async_remote_copy(
        src_ref=narrow_out,
        dst_ref=narrow_in,
        send_sem=narrow_sem.at[0],
        recv_sem=narrow_sem.at[1],
        device_id={"tp": column * 2 + 1 - side},
    )
    narrow_send.start()
    own = jnp.where(side == 0, left, right)
    narrow_send.wait_recv()
    attended[...] = (own + narrow_in[...].astype(F32)).astype(BF16)

    landing_load.wait()

    @pl.when(core == 0)
    def _():
        wait_bytes(forward_in.at[pl.ds(0, 46)], forward_sem.at[0])

    @pl.when(core == 1)
    def _():
        wait_bytes(forward_in.at[pl.ds(0, 47)], forward_sem.at[0])

    land_rows = iota((LAND_ROWS, LANE_ROWS), 0)
    land_cols = iota((LAND_ROWS, LANE_ROWS), 1)
    target_rows = iota((LAND_ROWS, 2 * HEAD_DIM), 0)
    for m in range(MOVING):
        first = copied[0, m]
        total_in = meta[me, MOVING + m]
        arrived = jnp.concatenate(
            [
                jnp.concatenate(
                    [forward_in[m * 12 + 2 * r], forward_in[m * 12 + 2 * r + 1]], axis=1
                )
                for r in range(6)
            ],
            axis=0,
        )
        place = (land_rows - land_cols == first).astype(F32).astype(BF16)
        placed = jnp.dot(place, arrived, preferred_element_type=F32).astype(BF16)
        fits = (target_rows >= first) & (target_rows < first + total_in)
        landed[m] = jnp.where(fits, placed, landing[m])

    for copy in wide_sends:
        copy.wait_send()
    narrow_send.wait_send()
    wait_bytes(scatter_out.at[pl.ds(0, 45)], scatter_sem.at[1])

    @pl.when(core == 0)
    def _():
        wait_bytes(scatter_out.at[pl.ds(0, 1)], scatter_sem.at[2])
        wait_bytes(forward_out.at[pl.ds(0, INSTS - 1)], forward_sem.at[1])

    @pl.when(core == 1)
    def _():
        wait_bytes(scatter_out.at[pl.ds(0, 2)], scatter_sem.at[2])
        wait_bytes(forward_out.at[pl.ds(0, INSTS - 1), 0], forward_sem.at[1])


def on_device(
    queries,
    key_values,
    new_key_values,
    cache_lengths,
    output_weight,
    moving_requests,
    migration_plan,
    row_counts,
    copied_rows,
    landing,
):
    in_hbm = pl.BlockSpec(memory_space=pltpu.HBM)
    dma = pltpu.SemaphoreType.DMA
    attended, landed = pl.pallas_call(
        main_kernel,
        out_shape=(
            jax.ShapeDtypeStruct((TOKENS, NARROW), BF16),
            jax.ShapeDtypeStruct((MOVING, LAND_ROWS, 2 * HEAD_DIM), BF16),
        ),
        in_specs=[in_hbm] * 10,
        out_specs=(
            pl.BlockSpec(memory_space=pltpu.VMEM),
            pl.BlockSpec(memory_space=pltpu.VMEM),
        ),
        scratch_shapes=[
            pltpu.SMEM((REQS,), I32),
            pltpu.SMEM((1, MOVING), I32),
            pltpu.SMEM((1, MOVING), I32),
            pltpu.VMEM((STEPS, REQS, HEADS * HEAD_DIM), BF16),
            pltpu.VMEM((TOKENS, 2 * HEAD_DIM), BF16),
            pltpu.VMEM((REQS * TILES, TILE, 2 * HEAD_DIM), BF16),
            pltpu.VMEM((4, HEADS * HEAD_DIM, WIDE), BF16),
            pltpu.VMEM((MOVING, INSTS), I32),
            pltpu.VMEM((STEPS, MOVING, INSTS), I32),
            pltpu.VMEM((MOVING, LAND_ROWS, 2 * HEAD_DIM), BF16),
            pltpu.VMEM((40, 128), I32),
            pltpu.SMEM((40, 128), I32),
            pltpu.VMEM((REQS * ROWS, HEAD_DIM), F32),
            pltpu.VMEM((REQS * ROWS, REQS * ROWS), BF16),
            pltpu.VMEM((REQS * ROWS, TOKENS), F32),
            pltpu.VMEM((REQS * ROWS, HEAD_DIM), F32),
            pltpu.VMEM((REQS * ROWS, HEAD_DIM), F32),
            pltpu.VMEM((REQS * ROWS, HEAD_DIM), F32),
            pltpu.VMEM((48, 16, 128), BF16),
            pltpu.VMEM((INSTS, 2, 16, 128), BF16),
            pltpu.VMEM((INSTS, 2, 16, 128), BF16),
            pltpu.VMEM((48, 16, 128), BF16),
            pltpu.VMEM((3, TOKENS, WIDE), BF16),
            pltpu.VMEM((3, TOKENS, WIDE), BF16),
            pltpu.VMEM((TOKENS, WIDE), F32),
            pltpu.VMEM((TOKENS, NARROW), BF16),
            pltpu.VMEM((TOKENS, NARROW), BF16),
            dma((7,)),
            dma((GROUPS,)),
            dma((4,)),
            dma((1,)),
            dma((1,)),
            dma((3,)),
            dma((2,)),
            dma((3,)),
            dma((3,)),
            dma((2,)),
        ],
        compiler_params=pltpu.CompilerParams(
            collective_id=0,
            has_side_effects=True,
            vmem_limit_bytes=40 * 1024 * 1024,
        ),
    )(
        *(
            pltpu.with_memory_space_constraint(x, pltpu.HBM)
            for x in (
                cache_lengths,
                moving_requests,
                copied_rows,
                queries,
                new_key_values.reshape(TOKENS, 2 * HEAD_DIM),
                key_values.reshape(REQS * TILES, TILE, 2 * HEAD_DIM),
                output_weight,
                migration_plan.T,
                row_counts.transpose(0, 2, 1),
                landing[0],
            )
        )
    )
    return attended.reshape(STEPS, REQS, NARROW), landed[None]


def solution(mesh):
    placed = (
        P(None, "inst", "tp"),
        P("inst", None, "tp"),
        P(None, "inst", "tp"),
        P("inst"),
        P("tp", None),
        P("inst", None),
        P(),
        P(),
        P("inst", None),
        P("inst", None, None, "tp"),
    )
    return jax.shard_map(
        on_device,
        mesh=mesh,
        in_specs=placed,
        out_specs=(P(None, "inst", "tp"), P("inst", None, None, "tp")),
        check_vma=False,
    )
```

time: 261 us -> 30.2 us (0.12)
  waiting for transfers between devices: 161 us -> 0 us
  local copies, waits for them, and re-layouts: 53.7 us -> 1.42 us
  Pallas kernels: 0 us -> 28.1 us
  matrix products: 26.2 us -> 0 us
  between operations: 16 us -> 0.64 us
  other arithmetic: 3.31 us -> 0 us
    all_gather x3 -> x0, waiting for transfers between devices: 133 us -> none  [on_device(): everyone = lax.all_gather(pieces[None], 'inst', axis=0, tiled=True)]
    pallas_call x0 -> x1, Pallas kernels: none -> 28.1 us  [on_device(): pl.pallas_call(main_kernel, out_shape=(jax.ShapeDtypeStruct((TOKENS, NARR...]
    reduce_scatter x1 -> x0, waiting for transfers between devices: 27.6 us -> none  [on_device(): lax.psum_scatter(partial_sums, 'tp', scatter_dimension=2, tiled=True)]
    dot_general x13 -> x0, matrix products: 26.2 us -> none  [the longest x3 10.3 us: attend(): jnp.einsum('sbkgl,blkd->sbkgd', old_weight, stored[:, :, :, 1], preferred...]
    scatter x3 -> x0, local copies, waits for them, and re-layouts: 22.1 us -> none  [place_rows(): return slots.at[lane_ids, position].set(arrived, mode='drop')]
    gather x6 -> x0, local copies, waits for them, and re-layouts: 16.9 us -> none  [the longest x1 9.22 us: tail_rows(): return key_values[chosen[:, None, None], positions]]
    unnamed x24 -> x2, local copies, waits for them, and re-layouts: 13.3 us -> 1.42 us
  transfers between devices with their start and end apart: 4 -> 0, of which waited for: 4 -> 0; matrix products, arithmetic and copies ran while one was open for 7% -> 0% of each run, Pallas kernels for 0% -> 0%
where the time goes in v1:
time: 30.2 us; the launch traced here: 30.1 us
  Pallas kernels  28.1 us (93%)
  local copies, waits for them, and re-layouts  1.42 us (5%)
  between operations  0.64 us (2%)
    pallas_call x1, Pallas kernels, on_device(): pl.pallas_call(main_kernel, out_shape=(jax.ShapeDtypeStruct((TOKENS, NARR...  28.1 us
    unnamed x2, local copies, waits for them, and re-layouts  1.42 us

profile of v1, /device:TPU:1, one launch (start us, length us, event | category | flops | bytes accessed | tf_op | source)
XLA Modules:
  0.0 30.1 jit_solution(1332187321072604322)
XLA Ops:
  0.6 28.1 %shard_map.113 = (bf16[48,512]{1,0:T(8,128)(2,1)S(1)}, bf16[4,256,256]{2,1,0:T(8,128)(2,1)S(1)}) custom-call(s32[16]{0:T(128)} %lengths_hbm.1, s32[1,4]{1,0:T(1,128)} %moving_hbm.1, s32[1,4]{1,0:T(1,128)} %copied_hbm.1, bf16[3,16,1024]{2,1,0:T(8,128)(2,1)} %queries_hbm.1, bf16[48,256]{1,0:T(8,128)(2,1)} %bitcast.11, bf16[1024,16,256]{2,1,0:T(8,128)(2,1)} %bitcast.9, ...), custom_call_target="tpu_custom_call" | custom-call | tf_op jit(solution)/shard_map/pallas_call | solution.py:463
  28.7 0.6 %copy.14 = bf16[3,16,512]{2,1,0:T(8,128)(2,1)} copy(bf16[3,16,512]{2,1,0:T(8,128)(2,1)S(1)} %bitcast.8) | data formatting | bytes 98304
  29.4 0.8 %copy.15 = bf16[1,4,256,256]{3,2,1,0:T(8,128)(2,1)} copy(bf16[1,4,256,256]{3,2,1,0:T(8,128)(2,1)S(1)} %bitcast.7) | data formatting | bytes 1048576

commit v2 on v1

--- a/solution.py
+++ b/solution.py
@@ -18,7 +18,8 @@
 LANE_ROWS = STEPS * MOST_ROWS
 LAND_ROWS = 256
 INSTS = 32
-CHIPS = 16
+PLANE = 8
+HALF = LANE_ROWS // 2
 TP = 8
 OUT_WIDTH = 4096
 ROWS = STEPS * HEADS
@@ -76,10 +77,12 @@
     acc,
     top,
     norm,
-    scatter_out,
-    scatter_in,
-    forward_out,
-    forward_in,
+    tails,
+    held,
+    inside,
+    upward,
+    downward,
+    arrived,
     wide_out,
     wide_in,
     wide_own,
@@ -98,19 +101,38 @@
 ):
     me = lax.axis_index("inst")
     tp = lax.axis_index("tp")
-    chip = me // 2
-    core = lax.rem(me, 2)
+    depth = lax.rem(me // 2, 4)
+    spot = (me // 8) * 2 + lax.rem(me, 2)
+    lane = me // 8
     column = tp // 2
     side = lax.rem(tp, 2)
-    lane = chip // 4
+
+    def device(place, plane):
+        return ((place // 2) * 4 + plane) * 2 + lax.rem(place, 2)
+
+    above, below = lax.rem(depth + 1, 4), lax.rem(depth + 3, 4)
 
     barrier = pltpu.get_barrier_semaphore()
 
     def greet(o, carry):
-        pl.semaphore_signal(
-            barrier, inc=1, device_id={"inst": lax.rem(me + o, INSTS)}
-        )
+        place = lax.rem(spot + o, PLANE)
+        for plane in (above, below):
+            pl.semaphore_signal(
+                barrier, inc=1, device_id={"inst": device(place, plane)}
+            )
         return carry
+
+    def greet_plane(o, carry):
+        place = lax.rem(spot + o, PLANE)
+        pl.semaphore_signal(barrier, inc=1, device_id={"inst": device(place, depth)})
+        return carry
+
+    lax.fori_loop(0, PLANE, greet, 0)
+    lax.fori_loop(1, PLANE, greet_plane, 0)
+    for k in range(3):
+        other = lax.rem(column + 1 + k, 4)
+        pl.semaphore_signal(barrier, inc=1, device_id={"tp": other * 2 + side})
+    pl.semaphore_signal(barrier, inc=1, device_id={"tp": column * 2 + 1 - side})
 
     small = [
         pltpu.make_async_copy(src, dst, small_sem.at[n])
@@ -135,11 +157,6 @@
             pltpu.make_async_copy(cache_hbm.at[part], cache.at[part], cache_sem.at[g])
         )
         cache_loads[-1].start()
-    lax.fori_loop(1, INSTS, greet, 0)
-    for k in range(3):
-        other = lax.rem(column + 1 + k, 4)
-        pl.semaphore_signal(barrier, inc=1, device_id={"tp": other * 2 + side})
-    pl.semaphore_signal(barrier, inc=1, device_id={"tp": column * 2 + 1 - side})
     weight_loads = []
     for k in range(4):
         target = lax.rem(column + 1 + k, 4)
@@ -150,9 +167,7 @@
                 weight_sem.at[k],
             )
         )
-        weight_loads[-1].start()
     landing_load = pltpu.make_async_copy(landing_hbm, landing, landing_sem.at[0])
-    landing_load.start()
 
     for copy in small:
         copy.wait()
@@ -162,10 +177,25 @@
     for m in range(MOVING):
         hit = plan[m : m + 1, :] == inst_rows
         sender = jnp.sum(jnp.where(hit, inst_cols, 0), axis=1, keepdims=True)
-        meta_vec[0:INSTS, m : m + 1] = jnp.minimum(sender, INSTS - 1)
-        meta_vec[0:INSTS, MOVING + m : MOVING + m + 1] = jnp.sum(
-            jnp.where(hit, total[m : m + 1, :], 0), axis=1, keepdims=True
-        )
+        sender = jnp.minimum(sender, INSTS - 1)
+        place = ((sender >> 3) << 1) + (sender & 1)
+        plane = (sender >> 1) & 3
+        offset = (plane - depth) & 3
+        away = (plane - ((inst_rows[:, :1] >> 1) & 3)) & 3
+        low, high = 2 * place, 2 * place + 1
+        from_below, from_above = 2 * PLANE + place, 3 * PLANE + place
+        columns = (
+            jnp.where(offset == 3, from_below, low),
+            jnp.where(offset == 1, from_above, high),
+            jnp.where(offset == 3, from_below, high),
+            jnp.where(offset == 1, from_above, low),
+            jnp.sum(jnp.where(hit, total[m : m + 1, :], 0), axis=1, keepdims=True),
+            jnp.where(away == 1, 3, jnp.where(away == 2, 2, 0)),
+            jnp.where(away == 3, 2, jnp.where(away == 2, 3, 1)),
+        )
+        for n, values in enumerate(columns):
+            n = n * MOVING + m
+            meta_vec[0:INSTS, n : n + 1] = values
     meta_vec[INSTS : INSTS + MOVING, 0:INSTS] = total
     meta_load = pltpu.make_async_copy(meta_vec, meta, meta_sem.at[0])
     meta_load.start()
@@ -240,6 +270,10 @@
 
     for g in range(GROUPS - 1):
         cache_loads[g].wait()
+        if g == 1:
+            for load in weight_loads:
+                load.start()
+            landing_load.start()
         attend_group(g)
     cache_loads[GROUPS - 1].wait()
 
@@ -258,47 +292,37 @@
         tail = jnp.dot(
             shift.astype(F32).astype(BF16), window, preferred_element_type=F32
         ).astype(BF16)
-        for q in range(12):
-            r, c = (q // 2) * 16, (q % 2) * 128
-            scatter_out[m * 12 + q] = tail[r : r + 16, c : c + 128]
-
-    pl.semaphore_wait(barrier, INSTS - 1 + 3 + 1)
-
-    def scatter_two(target_chip, sem):
-        return pltpu.make_async_remote_copy(
-            src_ref=scatter_out.at[pl.ds(target_chip * 3, 2)],
-            dst_ref=scatter_in.at[me],
-            send_sem=sem,
-            recv_sem=scatter_sem.at[0],
-            device_id={"inst": target_chip * 2},
-        )
-
-    def scatter_one(target_chip, sem):
-        return pltpu.make_async_remote_copy(
-            src_ref=scatter_out.at[pl.ds(target_chip * 3 + 2, 1)],
-            dst_ref=scatter_in.at[me, pl.ds(0, 1)],
-            send_sem=sem,
-            recv_sem=scatter_sem.at[0],
-            device_id={"inst": target_chip * 2 + 1},
-        )
+        for c in range(2):
+            for n in range(2):
+                tails[2 * m + c, n] = tail[
+                    n * HALF : (n + 1) * HALF, c * HEAD_DIM : (c + 1) * HEAD_DIM
+                ]
+
+    pl.semaphore_wait(barrier, 3 * PLANE - 1 + 3 + 1)
+
+    def send(src, dst, place, plane, sems):
+        pltpu.make_async_remote_copy(
+            src_ref=src,
+            dst_ref=dst,
+            send_sem=sems.at[0],
+            recv_sem=sems.at[1],
+            device_id={"inst": device(place, plane)},
+        ).start()
 
     def scatter(o, carry):
-        target_chip = lax.rem(chip + o, CHIPS)
-        scatter_two(target_chip, scatter_sem.at[1]).start()
-        scatter_one(target_chip, scatter_sem.at[1]).start()
+        place = lax.rem(spot + o, PLANE)
+        send(tails.at[place, 0], held.at[2 * PLANE + spot], place, above, scatter_sem)
+        send(tails.at[place, 1], held.at[3 * PLANE + spot], place, below, scatter_sem)
         return carry
 
-    lax.fori_loop(1, CHIPS, scatter, 0)
-
-    @pl.when(core == 0)
-    def _():
-        scatter_one(chip, scatter_sem.at[2]).start()
-        scatter_in[me] = scatter_out[pl.ds(chip * 3, 2)]
-
-    @pl.when(core == 1)
-    def _():
-        scatter_two(chip, scatter_sem.at[2]).start()
-        scatter_in[me, 0] = scatter_out[chip * 3 + 2]
+    def scatter_plane(o, carry):
+        place = lax.rem(spot + o, PLANE)
+        send(tails.at[place], held.at[pl.ds(2 * spot, 2)], place, depth, scatter_sem)
+        return carry
+
+    lax.fori_loop(0, PLANE, scatter, 0)
+    lax.fori_loop(1, PLANE, scatter_plane, 0)
+    held[pl.ds(2 * spot, 2)] = tails[spot]
 
     attend_group(GROUPS - 1)
 
@@ -335,51 +359,30 @@
     for k in range(4):
         project(k)
 
-    def forward_two(target):
-        return pltpu.make_async_remote_copy(
-            src_ref=forward_out.at[target],
-            dst_ref=forward_in.at[pl.ds(chip * 3, 2)],
-            send_sem=forward_sem.at[1],
-            recv_sem=forward_sem.at[0],
-            device_id={"inst": target},
-        )
-
-    def forward_one(target):
-        return pltpu.make_async_remote_copy(
-            src_ref=forward_out.at[target, pl.ds(0, 1)],
-            dst_ref=forward_in.at[pl.ds(chip * 3 + 2, 1)],
-            send_sem=forward_sem.at[1],
-            recv_sem=forward_sem.at[0],
-            device_id={"inst": target},
-        )
-
-    @pl.when(core == 0)
-    def _():
-        wait_bytes(scatter_in.at[pl.ds(0, INSTS - 1)], scatter_sem.at[0])
-
-        for d in range(INSTS):
-            forward_out[d] = scatter_in[meta[d, lane]]
-
-        def forward(o, carry):
-            forward_two(lax.rem(me + o, INSTS)).start()
-            return carry
-
-        lax.fori_loop(1, INSTS, forward, 0)
-        forward_in[pl.ds(chip * 3, 2)] = scatter_in[meta[me, lane]]
-
-    @pl.when(core == 1)
-    def _():
-        wait_bytes(scatter_in.at[pl.ds(0, INSTS - 1), 0], scatter_sem.at[0])
-
-        for d in range(INSTS):
-            forward_out[d, 0] = scatter_in[meta[d, lane], 0]
-
-        def forward(o, carry):
-            forward_one(lax.rem(me + o, INSTS)).start()
-            return carry
-
-        lax.fori_loop(1, INSTS, forward, 0)
-        forward_in[chip * 3 + 2] = scatter_in[meta[me, lane], 0]
+    wait_bytes(held.at[pl.ds(0, 4 * PLANE - 2)], scatter_sem.at[1])
+    for place in range(PLANE):
+        row = device(place, above)
+        upward[place] = held[meta[row, 2 * MOVING + lane]]
+        row = device(place, below)
+        downward[place] = held[meta[row, 3 * MOVING + lane]]
+        row = device(place, depth)
+        inside[place, 0] = held[meta[row, lane]]
+        inside[place, 1] = held[meta[row, MOVING + lane]]
+
+    def forward(o, carry):
+        place = lax.rem(spot + o, PLANE)
+        send(upward.at[place], arrived.at[4 * spot + 2], place, above, forward_sem)
+        send(downward.at[place], arrived.at[4 * spot + 3], place, below, forward_sem)
+        return carry
+
+    def forward_plane(o, carry):
+        place = lax.rem(spot + o, PLANE)
+        send(inside.at[place], arrived.at[pl.ds(4 * spot, 2)], place, depth, forward_sem)
+        return carry
+
+    lax.fori_loop(0, PLANE, forward, 0)
+    lax.fori_loop(1, PLANE, forward_plane, 0)
+    arrived[pl.ds(4 * spot, 2)] = inside[spot]
 
     for k in range(3):
         pltpu.make_async_copy(wide_in.at[k], wide_in.at[k], wide_recv_sem.at[k]).wait()
@@ -402,48 +405,48 @@
 
     landing_load.wait()
 
-    @pl.when(core == 0)
-    def _():
-        wait_bytes(forward_in.at[pl.ds(0, 46)], forward_sem.at[0])
-
-    @pl.when(core == 1)
-    def _():
-        wait_bytes(forward_in.at[pl.ds(0, 47)], forward_sem.at[0])
+    wait_bytes(arrived.at[pl.ds(0, 4 * PLANE - 2)], forward_sem.at[1])
 
     land_rows = iota((LAND_ROWS, LANE_ROWS), 0)
     land_cols = iota((LAND_ROWS, LANE_ROWS), 1)
     target_rows = iota((LAND_ROWS, 2 * HEAD_DIM), 0)
     for m in range(MOVING):
         first = copied[0, m]
-        total_in = meta[me, MOVING + m]
-        arrived = jnp.concatenate(
+        total_in = meta[me, 4 * MOVING + m]
+        rows = jnp.concatenate(
             [
                 jnp.concatenate(
-                    [forward_in[m * 12 + 2 * r], forward_in[m * 12 + 2 * r + 1]], axis=1
+                    [
+                        arrived[(2 * m + c) * 4 + meta[me, (5 + n) * MOVING + m]]
+                        for c in range(2)
+                    ],
+                    axis=1,
                 )
-                for r in range(6)
+                for n in range(2)
             ],
             axis=0,
         )
         place = (land_rows - land_cols == first).astype(F32).astype(BF16)
-        placed = jnp.dot(place, arrived, preferred_element_type=F32).astype(BF16)
+        placed = jnp.dot(place, rows, preferred_element_type=F32).astype(BF16)
         fits = (target_rows >= first) & (target_rows < first + total_in)
         landed[m] = jnp.where(fits, placed, landing[m])
 
     for copy in wide_sends:
         copy.wait_send()
     narrow_send.wait_send()
-    wait_bytes(scatter_out.at[pl.ds(0, 45)], scatter_sem.at[1])
-
-    @pl.when(core == 0)
-    def _():
-        wait_bytes(scatter_out.at[pl.ds(0, 1)], scatter_sem.at[2])
-        wait_bytes(forward_out.at[pl.ds(0, INSTS - 1)], forward_sem.at[1])
-
-    @pl.when(core == 1)
-    def _():
-        wait_bytes(scatter_out.at[pl.ds(0, 2)], scatter_sem.at[2])
-        wait_bytes(forward_out.at[pl.ds(0, INSTS - 1), 0], forward_sem.at[1])
+    wait_bytes(held.at[pl.ds(0, 4 * PLANE - 2)], scatter_sem.at[0])
+    wait_bytes(arrived.at[pl.ds(0, 4 * PLANE - 2)], forward_sem.at[0])
+
+
+def publish(attended, landed, attended_out, landed_out, sems):
+    copies = [pltpu.make_async_copy(attended, attended_out, sems.at[MOVING])] + [
+        pltpu.make_async_copy(landed.at[m], landed_out.at[m], sems.at[m])
+        for m in range(MOVING)
+    ]
+    for copy in copies:
+        copy.start()
+    for copy in copies:
+        copy.wait()
 
 
 def on_device(
@@ -490,10 +493,12 @@
             pltpu.VMEM((REQS * ROWS, HEAD_DIM), F32),
             pltpu.VMEM((REQS * ROWS, HEAD_DIM), F32),
             pltpu.VMEM((REQS * ROWS, HEAD_DIM), F32),
-            pltpu.VMEM((48, 16, 128), BF16),
-            pltpu.VMEM((INSTS, 2, 16, 128), BF16),
-            pltpu.VMEM((INSTS, 2, 16, 128), BF16),
-            pltpu.VMEM((48, 16, 128), BF16),
+            pltpu.VMEM((PLANE, 2, HALF, HEAD_DIM), BF16),
+            pltpu.VMEM((4 * PLANE, HALF, HEAD_DIM), BF16),
+            pltpu.VMEM((PLANE, 2, HALF, HEAD_DIM), BF16),
+            pltpu.VMEM((PLANE, HALF, HEAD_DIM), BF16),
+            pltpu.VMEM((PLANE, HALF, HEAD_DIM), BF16),
+            pltpu.VMEM((4 * PLANE, HALF, HEAD_DIM), BF16),
             pltpu.VMEM((3, TOKENS, WIDE), BF16),
             pltpu.VMEM((3, TOKENS, WIDE), BF16),
             pltpu.VMEM((TOKENS, WIDE), F32),
@@ -504,7 +509,7 @@
             dma((4,)),
             dma((1,)),
             dma((1,)),
-            dma((3,)),
+            dma((2,)),
             dma((2,)),
             dma((3,)),
             dma((3,)),
@@ -532,6 +537,22 @@
             )
         )
     )
+    in_vmem = pl.BlockSpec(memory_space=pltpu.VMEM)
+    anywhere = pl.BlockSpec(memory_space=pl.ANY)
+    attended, landed = pl.pallas_call(
+        publish,
+        out_shape=(
+            jax.ShapeDtypeStruct(attended.shape, BF16),
+            jax.ShapeDtypeStruct(landed.shape, BF16),
+        ),
+        in_specs=[in_vmem, in_vmem],
+        out_specs=(anywhere, anywhere),
+        scratch_shapes=[dma((MOVING + 1,))],
+        compiler_params=pltpu.CompilerParams(vmem_limit_bytes=4 * 1024 * 1024),
+    )(
+        pltpu.with_memory_space_constraint(attended, pltpu.VMEM),
+        pltpu.with_memory_space_constraint(landed, pltpu.VMEM),
+    )
     return attended.reshape(STEPS, REQS, NARROW), landed[None]
 
 

time: 30.2 us -> 28.3 us (0.937)
  local copies, waits for them, and re-layouts: 1.42 us -> 0 us
  Pallas kernels: 28.1 us -> 27.6 us
    unnamed x2 -> x0, local copies, waits for them, and re-layouts: 1.42 us -> none
    pallas_call x1, Pallas kernels: 28.1 us -> 26.8 us  [on_device(): pl.pallas_call(main_kernel, out_shape=(jax.ShapeDtypeStruct((TOKENS, NARR...]
    pallas_call x0 -> x1, Pallas kernels: none -> 0.85 us  [on_device(): pl.pallas_call(publish, out_shape=(jax.ShapeDtypeStruct(attended.shape, B...]
where the time goes in v2:
time: 28.3 us
  Pallas kernels  27.6 us (98%)
  between operations  0.64 us (2%)
    pallas_call x1, Pallas kernels, on_device(): pl.pallas_call(main_kernel, out_shape=(jax.ShapeDtypeStruct((TOKENS, NARR...  26.8 us
    pallas_call x1, Pallas kernels, on_device(): pl.pallas_call(publish, out_shape=(jax.ShapeDtypeStruct(attended.shape, B...  0.85 us

profile of v2, /device:TPU:1, one launch (start us, length us, event | category | flops | bytes accessed | tf_op | source)
XLA Modules:
  0.0 28.3 jit_solution(17197708963789221809)
XLA Ops:
  0.6 26.8 %shard_map.113 = (bf16[48,512]{1,0:T(8,128)(2,1)S(1)}, bf16[4,256,256]{2,1,0:T(8,128)(2,1)S(1)}) custom-call(s32[16]{0:T(128)} %lengths_hbm.1, s32[1,4]{1,0:T(1,128)} %moving_hbm.1, s32[1,4]{1,0:T(1,128)} %copied_hbm.1, bf16[3,16,1024]{2,1,0:T(8,128)(2,1)} %queries_hbm.1, bf16[48,256]{1,0:T(8,128)(2,1)} %bitcast.9, bf16[1024,16,256]{2,1,0:T(8,128)(2,1)} %bitcast.7, ...), custom_call_target="tpu_custom_call" | custom-call | tf_op jit(solution)/shard_map/pallas_call | solution.py:466
  27.4 0.8 %shard_map.114 = (bf16[48,512]{1,0:T(8,128)(2,1)}, bf16[4,256,256]{2,1,0:T(8,128)(2,1)}) custom-call(bf16[48,512]{1,0:T(8,128)(2,1)S(1)} %get-tuple-element.6.attended, bf16[4,256,256]{2,1,0:T(8,128)(2,1)S(1)} %get-tuple-element.7.landed), custom_call_target="tpu_custom_call" | custom-call | tf_op jit(solution)/shard_map/pallas_call | solution.py:542

commit v3 on v2

--- a/solution.py
+++ b/solution.py
@@ -20,6 +20,7 @@
 INSTS = 32
 PLANE = 8
 HALF = LANE_ROWS // 2
+BATCHES = HALF // 16
 TP = 8
 OUT_WIDTH = 4096
 ROWS = STEPS * HEADS
@@ -75,10 +76,12 @@
     regroup,
     new_scores,
     acc,
-    top,
-    norm,
+    shifts,
+    places,
     tails,
-    held,
+    held_0,
+    held_1,
+    held_2,
     inside,
     upward,
     downward,
@@ -111,6 +114,7 @@
         return ((place // 2) * 4 + plane) * 2 + lax.rem(place, 2)
 
     above, below = lax.rem(depth + 1, 4), lax.rem(depth + 3, 4)
+    held = (held_0, held_1, held_2)
 
     barrier = pltpu.get_barrier_semaphore()
 
@@ -258,15 +262,30 @@
             for r, x in zip(rows, scores)
         ]
         weights = [jnp.exp2(x - h) for x, h in zip(scores, highest)]
-        sums = [jnp.sum(w, axis=1, keepdims=True) for w in weights]
+        late = [jnp.exp2(new_scores[r, :] - h) for r, h in zip(rows, highest)]
+        shares = [
+            1.0 / (jnp.sum(w, axis=1, keepdims=True) + jnp.sum(n, axis=1, keepdims=True))
+            for w, n in zip(weights, late)
+        ]
         outs = [
-            jnp.dot(w.astype(BF16), kv[:, HEAD_DIM:], preferred_element_type=F32)
-            for w, kv in zip(weights, stored)
+            jnp.dot((w * x).astype(BF16), kv[:, HEAD_DIM:], preferred_element_type=F32)
+            for w, x, kv in zip(weights, shares, stored)
         ]
-        for r, h, n, o in zip(rows, highest, sums, outs):
-            top[r, :] = jnp.broadcast_to(h, (ROWS, HEAD_DIM))
-            norm[r, :] = jnp.broadcast_to(n, (ROWS, HEAD_DIM))
+        for r, n, x, o in zip(rows, late, shares, outs):
+            new_scores[r, :] = n * x
             acc[r, :] = o
+
+    meta_load.wait()
+    tail_rows = iota((LANE_ROWS, WINDOW), 0)
+    tail_cols = iota((LANE_ROWS, WINDOW), 1)
+    first_tiles = []
+    for m in range(MOVING):
+        total = meta[INSTS + m, me]
+        start = lengths[moving[0, m]] - total
+        first = jnp.minimum(start // TILE, TILES - WINDOW // TILE)
+        first_tiles.append(first)
+        shift = (tail_cols - tail_rows == start - first * TILE) & (tail_rows < total)
+        shifts[m] = shift.astype(F32).astype(BF16)
 
     for g in range(GROUPS - 1):
         cache_loads[g].wait()
@@ -277,61 +296,77 @@
         attend_group(g)
     cache_loads[GROUPS - 1].wait()
 
-    meta_load.wait()
-    tail_rows = iota((LANE_ROWS, WINDOW), 0)
-    tail_cols = iota((LANE_ROWS, WINDOW), 1)
     for m in range(MOVING):
-        request = moving[0, m]
-        total = meta[INSTS + m, me]
-        start = lengths[request] - total
-        first = jnp.minimum(start // TILE, TILES - WINDOW // TILE)
+        tile = moving[0, m] * TILES + first_tiles[m]
         window = jnp.concatenate(
-            [cache[request * TILES + first + t] for t in range(WINDOW // TILE)], axis=0
+            [cache[tile + t] for t in range(WINDOW // TILE)], axis=0
         )
-        shift = (tail_cols - tail_rows == start - first * TILE) & (tail_rows < total)
-        tail = jnp.dot(
-            shift.astype(F32).astype(BF16), window, preferred_element_type=F32
-        ).astype(BF16)
+        tail = jnp.dot(shifts[m], window, preferred_element_type=F32).astype(BF16)
         for c in range(2):
             for n in range(2):
-                tails[2 * m + c, n] = tail[
-                    n * HALF : (n + 1) * HALF, c * HEAD_DIM : (c + 1) * HEAD_DIM
-                ]
+                for t in range(BATCHES):
+                    first_row = n * HALF + t * TILE
+                    tails[t, 2 * m + c, n] = tail[
+                        first_row : first_row + TILE, c * HEAD_DIM : (c + 1) * HEAD_DIM
+                    ]
 
     pl.semaphore_wait(barrier, 3 * PLANE - 1 + 3 + 1)
 
-    def send(src, dst, place, plane, sems):
+    def send(src, dst, place, plane, sems, t):
         pltpu.make_async_remote_copy(
             src_ref=src,
             dst_ref=dst,
-            send_sem=sems.at[0],
-            recv_sem=sems.at[1],
+            send_sem=sems.at[0, t],
+            recv_sem=sems.at[1, t],
             device_id={"inst": device(place, plane)},
         ).start()
 
-    def scatter(o, carry):
-        place = lax.rem(spot + o, PLANE)
-        send(tails.at[place, 0], held.at[2 * PLANE + spot], place, above, scatter_sem)
-        send(tails.at[place, 1], held.at[3 * PLANE + spot], place, below, scatter_sem)
-        return carry
-
-    def scatter_plane(o, carry):
-        place = lax.rem(spot + o, PLANE)
-        send(tails.at[place], held.at[pl.ds(2 * spot, 2)], place, depth, scatter_sem)
-        return carry
-
-    lax.fori_loop(0, PLANE, scatter, 0)
-    lax.fori_loop(1, PLANE, scatter_plane, 0)
-    held[pl.ds(2 * spot, 2)] = tails[spot]
+    def scatter(t):
+        def beside(o, carry):
+            place = lax.rem(spot + o, PLANE)
+            send(
+                tails.at[t, place, 0],
+                held[t].at[2 * PLANE + spot],
+                place,
+                above,
+                scatter_sem,
+                t,
+            )
+            send(
+                tails.at[t, place, 1],
+                held[t].at[3 * PLANE + spot],
+                place,
+                below,
+                scatter_sem,
+                t,
+            )
+            return carry
+
+        def within(o, carry):
+            place = lax.rem(spot + o, PLANE)
+            send(
+                tails.at[t, place],
+                held[t].at[pl.ds(2 * spot, 2)],
+                place,
+                depth,
+                scatter_sem,
+                t,
+            )
+            return carry
+
+        lax.fori_loop(0, PLANE, beside, 0)
+        lax.fori_loop(1, PLANE, within, 0)
+        held[t][pl.ds(2 * spot, 2)] = tails[t, spot]
+
+    for t in range(BATCHES):
+        scatter(t)
 
     attend_group(GROUPS - 1)
 
-    late = jnp.exp2(new_scores[...] - top[:, :TOKENS])
-    whole = norm[...] + jnp.sum(late, axis=1, keepdims=True)
     context = acc[...] + jnp.dot(
-        late.astype(BF16), newest[:, HEAD_DIM:], preferred_element_type=F32
-    )
-    context = (context / whole).astype(BF16)
+        new_scores[...].astype(BF16), newest[:, HEAD_DIM:], preferred_element_type=F32
+    )
+    context = context.astype(BF16)
     context = jnp.dot(regroup[...], context, preferred_element_type=F32).astype(BF16)
     context = jnp.concatenate(
         [context[h * TOKENS : (h + 1) * TOKENS] for h in range(HEADS)], axis=1
@@ -359,30 +394,67 @@
     for k in range(4):
         project(k)
 
-    wait_bytes(held.at[pl.ds(0, 4 * PLANE - 2)], scatter_sem.at[1])
-    for place in range(PLANE):
-        row = device(place, above)
-        upward[place] = held[meta[row, 2 * MOVING + lane]]
-        row = device(place, below)
-        downward[place] = held[meta[row, 3 * MOVING + lane]]
-        row = device(place, depth)
-        inside[place, 0] = held[meta[row, lane]]
-        inside[place, 1] = held[meta[row, MOVING + lane]]
-
-    def forward(o, carry):
-        place = lax.rem(spot + o, PLANE)
-        send(upward.at[place], arrived.at[4 * spot + 2], place, above, forward_sem)
-        send(downward.at[place], arrived.at[4 * spot + 3], place, below, forward_sem)
-        return carry
-
-    def forward_plane(o, carry):
-        place = lax.rem(spot + o, PLANE)
-        send(inside.at[place], arrived.at[pl.ds(4 * spot, 2)], place, depth, forward_sem)
-        return carry
-
-    lax.fori_loop(0, PLANE, forward, 0)
-    lax.fori_loop(1, PLANE, forward_plane, 0)
-    arrived[pl.ds(4 * spot, 2)] = inside[spot]
+    land_rows = iota((LAND_ROWS, LANE_ROWS), 0)
+    land_cols = iota((LAND_ROWS, LANE_ROWS), 1)
+    target_rows = iota((LAND_ROWS, 2 * HEAD_DIM), 0)
+    landing_load.wait()
+    for m in range(MOVING):
+        first = copied[0, m]
+        total_in = meta[me, 4 * MOVING + m]
+        place = (land_rows - land_cols == first) & (land_cols < total_in)
+        places[m] = place.astype(F32).astype(BF16)
+        fits = (target_rows >= first) & (target_rows < first + total_in)
+        landing[m] = jnp.where(fits, 0.0, landing[m].astype(F32)).astype(BF16)
+
+    def forward(t):
+        wait_bytes(held[t].at[pl.ds(0, 4 * PLANE - 2)], scatter_sem.at[1, t])
+        for place in range(PLANE):
+            row = device(place, above)
+            upward[t, place] = held[t][meta[row, 2 * MOVING + lane]]
+            row = device(place, below)
+            downward[t, place] = held[t][meta[row, 3 * MOVING + lane]]
+            row = device(place, depth)
+            inside[t, place, 0] = held[t][meta[row, lane]]
+            inside[t, place, 1] = held[t][meta[row, MOVING + lane]]
+
+        def beside(o, carry):
+            place = lax.rem(spot + o, PLANE)
+            send(
+                upward.at[t, place],
+                arrived.at[t, 4 * spot + 2],
+                place,
+                above,
+                forward_sem,
+                t,
+            )
+            send(
+                downward.at[t, place],
+                arrived.at[t, 4 * spot + 3],
+                place,
+                below,
+                forward_sem,
+                t,
+            )
+            return carry
+
+        def within(o, carry):
+            place = lax.rem(spot + o, PLANE)
+            send(
+                inside.at[t, place],
+                arrived.at[t, pl.ds(4 * spot, 2)],
+                place,
+                depth,
+                forward_sem,
+                t,
+            )
+            return carry
+
+        lax.fori_loop(0, PLANE, beside, 0)
+        lax.fori_loop(1, PLANE, within, 0)
+        arrived[t, pl.ds(4 * spot, 2)] = inside[t, spot]
+
+    for t in range(BATCHES):
+        forward(t)
 
     for k in range(3):
         pltpu.make_async_copy(wide_in.at[k], wide_in.at[k], wide_recv_sem.at[k]).wait()
@@ -403,39 +475,33 @@
     narrow_send.wait_recv()
     attended[...] = (own + narrow_in[...].astype(F32)).astype(BF16)
 
-    landing_load.wait()
-
-    wait_bytes(arrived.at[pl.ds(0, 4 * PLANE - 2)], forward_sem.at[1])
-
-    land_rows = iota((LAND_ROWS, LANE_ROWS), 0)
-    land_cols = iota((LAND_ROWS, LANE_ROWS), 1)
-    target_rows = iota((LAND_ROWS, 2 * HEAD_DIM), 0)
+    for t in range(BATCHES):
+        wait_bytes(arrived.at[t, pl.ds(0, 4 * PLANE - 2)], forward_sem.at[1, t])
+
     for m in range(MOVING):
-        first = copied[0, m]
-        total_in = meta[me, 4 * MOVING + m]
         rows = jnp.concatenate(
             [
                 jnp.concatenate(
                     [
-                        arrived[(2 * m + c) * 4 + meta[me, (5 + n) * MOVING + m]]
+                        arrived[t, (2 * m + c) * 4 + meta[me, (5 + n) * MOVING + m]]
                         for c in range(2)
                     ],
                     axis=1,
                 )
                 for n in range(2)
+                for t in range(BATCHES)
             ],
             axis=0,
         )
-        place = (land_rows - land_cols == first).astype(F32).astype(BF16)
-        placed = jnp.dot(place, rows, preferred_element_type=F32).astype(BF16)
-        fits = (target_rows >= first) & (target_rows < first + total_in)
-        landed[m] = jnp.where(fits, placed, landing[m])
+        placed = jnp.dot(places[m], rows, preferred_element_type=F32)
+        landed[m] = (landing[m].astype(F32) + placed).astype(BF16)
 
     for copy in wide_sends:
         copy.wait_send()
     narrow_send.wait_send()
-    wait_bytes(held.at[pl.ds(0, 4 * PLANE - 2)], scatter_sem.at[0])
-    wait_bytes(arrived.at[pl.ds(0, 4 * PLANE - 2)], forward_sem.at[0])
+    for t in range(BATCHES):
+        wait_bytes(held[t].at[pl.ds(0, 4 * PLANE - 2)], scatter_sem.at[0, t])
+        wait_bytes(arrived.at[t, pl.ds(0, 4 * PLANE - 2)], forward_sem.at[0, t])
 
 
 def publish(attended, landed, attended_out, landed_out, sems):
@@ -491,14 +557,16 @@
             pltpu.VMEM((REQS * ROWS, REQS * ROWS), BF16),
             pltpu.VMEM((REQS * ROWS, TOKENS), F32),
             pltpu.VMEM((REQS * ROWS, HEAD_DIM), F32),
-            pltpu.VMEM((REQS * ROWS, HEAD_DIM), F32),
-            pltpu.VMEM((REQS * ROWS, HEAD_DIM), F32),
-            pltpu.VMEM((PLANE, 2, HALF, HEAD_DIM), BF16),
-            pltpu.VMEM((4 * PLANE, HALF, HEAD_DIM), BF16),
-            pltpu.VMEM((PLANE, 2, HALF, HEAD_DIM), BF16),
-            pltpu.VMEM((PLANE, HALF, HEAD_DIM), BF16),
-            pltpu.VMEM((PLANE, HALF, HEAD_DIM), BF16),
-            pltpu.VMEM((4 * PLANE, HALF, HEAD_DIM), BF16),
+            pltpu.VMEM((MOVING, LANE_ROWS, WINDOW), BF16),
+            pltpu.VMEM((MOVING, LAND_ROWS, LANE_ROWS), BF16),
+            pltpu.VMEM((BATCHES, PLANE, 2, TILE, HEAD_DIM), BF16),
+            pltpu.VMEM((4 * PLANE, TILE, HEAD_DIM), BF16),
+            pltpu.VMEM((4 * PLANE, TILE, HEAD_DIM), BF16),
+            pltpu.VMEM((4 * PLANE, TILE, HEAD_DIM), BF16),
+            pltpu.VMEM((BATCHES, PLANE, 2, TILE, HEAD_DIM), BF16),
+            pltpu.VMEM((BATCHES, PLANE, TILE, HEAD_DIM), BF16),
+            pltpu.VMEM((BATCHES, PLANE, TILE, HEAD_DIM), BF16),
+            pltpu.VMEM((BATCHES, 4 * PLANE, TILE, HEAD_DIM), BF16),
             pltpu.VMEM((3, TOKENS, WIDE), BF16),
             pltpu.VMEM((3, TOKENS, WIDE), BF16),
             pltpu.VMEM((TOKENS, WIDE), F32),
@@ -509,8 +577,8 @@
             dma((4,)),
             dma((1,)),
             dma((1,)),
-            dma((2,)),
-            dma((2,)),
+            dma((2, BATCHES)),
+            dma((2, BATCHES)),
             dma((3,)),
             dma((3,)),
             dma((2,)),

time: 28.3 us -> 27.9 us (0.986)
  Pallas kernels: 27.6 us -> 27.2 us
    pallas_call x1, Pallas kernels: 26.8 us -> 26.3 us  [on_device(): pl.pallas_call(main_kernel, out_shape=(jax.ShapeDtypeStruct((TOKENS, NARR...]
where the time goes in v3:
time: 27.9 us; the launch traced here: 27.8 us
  Pallas kernels  27.2 us (97%)
  between operations  0.64 us (2%)
    pallas_call x1, Pallas kernels, on_device(): pl.pallas_call(main_kernel, out_shape=(jax.ShapeDtypeStruct((TOKENS, NARR...  26.3 us
    pallas_call x1, Pallas kernels, on_device(): pl.pallas_call(publish, out_shape=(jax.ShapeDtypeStruct(attended.shape, B...  0.85 us

profile of v3, /device:TPU:1, one launch (start us, length us, event | category | flops | bytes accessed | tf_op | source)
XLA Modules:
  0.0 27.8 jit_solution(13340785298891669648)
XLA Ops:
  0.6 26.3 %shard_map.113 = (bf16[48,512]{1,0:T(8,128)(2,1)S(1)}, bf16[4,256,256]{2,1,0:T(8,128)(2,1)S(1)}) custom-call(s32[16]{0:T(128)} %lengths_hbm.1, s32[1,4]{1,0:T(1,128)} %moving_hbm.1, s32[1,4]{1,0:T(1,128)} %copied_hbm.1, bf16[3,16,1024]{2,1,0:T(8,128)(2,1)} %queries_hbm.1, bf16[48,256]{1,0:T(8,128)(2,1)} %bitcast.9, bf16[1024,16,256]{2,1,0:T(8,128)(2,1)} %bitcast.7, ...), custom_call_target="tpu_custom_call" | custom-call | tf_op jit(solution)/shard_map/pallas_call | solution.py:532
  27.0 0.8 %shard_map.114 = (bf16[48,512]{1,0:T(8,128)(2,1)}, bf16[4,256,256]{2,1,0:T(8,128)(2,1)}) custom-call(bf16[48,512]{1,0:T(8,128)(2,1)S(1)} %get-tuple-element.6.attended, bf16[4,256,256]{2,1,0:T(8,128)(2,1)S(1)} %get-tuple-element.7.landed), custom_call_target="tpu_custom_call" | custom-call | tf_op jit(solution)/shard_map/pallas_call | solution.py:610

commit v4 on v3

--- a/solution.py
+++ b/solution.py
@@ -287,14 +287,15 @@
         shift = (tail_cols - tail_rows == start - first * TILE) & (tail_rows < total)
         shifts[m] = shift.astype(F32).astype(BF16)
 
-    for g in range(GROUPS - 1):
+    for g in range(1):
         cache_loads[g].wait()
-        if g == 1:
+        if g == 0:
             for load in weight_loads:
                 load.start()
             landing_load.start()
         attend_group(g)
-    cache_loads[GROUPS - 1].wait()
+    for g in range(1, GROUPS):
+        cache_loads[g].wait()
 
     for m in range(MOVING):
         tile = moving[0, m] * TILES + first_tiles[m]
@@ -361,7 +362,8 @@
     for t in range(BATCHES):
         scatter(t)
 
-    attend_group(GROUPS - 1)
+    for g in range(1, GROUPS):
+        attend_group(g)
 
     context = acc[...] + jnp.dot(
         new_scores[...].astype(BF16), newest[:, HEAD_DIM:], preferred_element_type=F32
@@ -394,6 +396,56 @@
     for k in range(4):
         project(k)
 
+    def forward(t):
+        wait_bytes(held[t].at[pl.ds(0, 4 * PLANE - 2)], scatter_sem.at[1, t])
+        for place in range(PLANE):
+            row = device(place, above)
+            upward[t, place] = held[t][meta[row, 2 * MOVING + lane]]
+            row = device(place, below)
+            downward[t, place] = held[t][meta[row, 3 * MOVING + lane]]
+            row = device(place, depth)
+            inside[t, place, 0] = held[t][meta[row, lane]]
+            inside[t, place, 1] = held[t][meta[row, MOVING + lane]]
+
+        def beside(o, carry):
+            place = lax.rem(spot + o, PLANE)
+            send(
+                upward.at[t, place],
+                arrived.at[t, 4 * spot + 2],
+                place,
+                above,
+                forward_sem,
+                t,
+            )
+            send(
+                downward.at[t, place],
+                arrived.at[t, 4 * spot + 3],
+                place,
+                below,
+                forward_sem,
+                t,
+            )
+            return carry
+
+        def within(o, carry):
+            place = lax.rem(spot + o, PLANE)
+            send(
+                inside.at[t, place],
+                arrived.at[t, pl.ds(4 * spot, 2)],
+                place,
+                depth,
+                forward_sem,
+                t,
+            )
+            return carry
+
+        lax.fori_loop(0, PLANE, beside, 0)
+        lax.fori_loop(1, PLANE, within, 0)
+        arrived[t, pl.ds(4 * spot, 2)] = inside[t, spot]
+
+    for t in range(BATCHES):
+        forward(t)
+
     land_rows = iota((LAND_ROWS, LANE_ROWS), 0)
     land_cols = iota((LAND_ROWS, LANE_ROWS), 1)
     target_rows = iota((LAND_ROWS, 2 * HEAD_DIM), 0)
@@ -405,56 +457,6 @@
         places[m] = place.astype(F32).astype(BF16)
         fits = (target_rows >= first) & (target_rows < first + total_in)
         landing[m] = jnp.where(fits, 0.0, landing[m].astype(F32)).astype(BF16)
-
-    def forward(t):
-        wait_bytes(held[t].at[pl.ds(0, 4 * PLANE - 2)], scatter_sem.at[1, t])
-        for place in range(PLANE):
-            row = device(place, above)
-            upward[t, place] = held[t][meta[row, 2 * MOVING + lane]]
-            row = device(place, below)
-            downward[t, place] = held[t][meta[row, 3 * MOVING + lane]]
-            row = device(place, depth)
-            inside[t, place, 0] = held[t][meta[row, lane]]
-            inside[t, place, 1] = held[t][meta[row, MOVING + lane]]
-
-        def beside(o, carry):
-            place = lax.rem(spot + o, PLANE)
-            send(
-                upward.at[t, place],
-                arrived.at[t, 4 * spot + 2],
-                place,
-                above,
-                forward_sem,
-                t,
-            )
-            send(
-                downward.at[t, place],
-                arrived.at[t, 4 * spot + 3],
-                place,
-                below,
-                forward_sem,
-                t,
-            )
-            return carry
-
-        def within(o, carry):
-            place = lax.rem(spot + o, PLANE)
-            send(
-                inside.at[t, place],
-                arrived.at[t, pl.ds(4 * spot, 2)],
-                place,
-                depth,
-                forward_sem,
-                t,
-            )
-            return carry
-
-        lax.fori_loop(0, PLANE, beside, 0)
-        lax.fori_loop(1, PLANE, within, 0)
-        arrived[t, pl.ds(4 * spot, 2)] = inside[t, spot]
-
-    for t in range(BATCHES):
-        forward(t)
 
     for k in range(3):
         pltpu.make_async_copy(wide_in.at[k], wide_in.at[k], wide_recv_sem.at[k]).wait()

time: 27.9 us -> 27.2 us (0.975)
  Pallas kernels: 27.2 us -> 26.4 us
    pallas_call x1, Pallas kernels: 26.3 us -> 25.6 us  [on_device(): pl.pallas_call(main_kernel, out_shape=(jax.ShapeDtypeStruct((TOKENS, NARR...]
where the time goes in v4:
time: 27.2 us; the launch traced here: 27.1 us
  Pallas kernels  26.4 us (97%)
  between operations  0.64 us (2%)
    pallas_call x1, Pallas kernels, on_device(): pl.pallas_call(main_kernel, out_shape=(jax.ShapeDtypeStruct((TOKENS, NARR...  25.6 us
    pallas_call x1, Pallas kernels, on_device(): pl.pallas_call(publish, out_shape=(jax.ShapeDtypeStruct(attended.shape, B...  0.85 us

profile of v4, /device:TPU:1, one launch (start us, length us, event | category | flops | bytes accessed | tf_op | source)
XLA Modules:
  0.0 27.1 jit_solution(6139239385799248722)
XLA Ops:
  0.6 25.6 %shard_map.113 = (bf16[48,512]{1,0:T(8,128)(2,1)S(1)}, bf16[4,256,256]{2,1,0:T(8,128)(2,1)S(1)}) custom-call(s32[16]{0:T(128)} %lengths_hbm.1, s32[1,4]{1,0:T(1,128)} %moving_hbm.1, s32[1,4]{1,0:T(1,128)} %copied_hbm.1, bf16[3,16,1024]{2,1,0:T(8,128)(2,1)} %queries_hbm.1, bf16[48,256]{1,0:T(8,128)(2,1)} %bitcast.9, bf16[1024,16,256]{2,1,0:T(8,128)(2,1)} %bitcast.7, ...), custom_call_target="tpu_custom_call" | custom-call | tf_op jit(solution)/shard_map/pallas_call | solution.py:534
  26.2 0.8 %shard_map.114 = (bf16[48,512]{1,0:T(8,128)(2,1)}, bf16[4,256,256]{2,1,0:T(8,128)(2,1)}) custom-call(bf16[48,512]{1,0:T(8,128)(2,1)S(1)} %get-tuple-element.6.attended, bf16[4,256,256]{2,1,0:T(8,128)(2,1)S(1)} %get-tuple-element.7.landed), custom_call_target="tpu_custom_call" | custom-call | tf_op jit(solution)/shard_map/pallas_call | solution.py:612

commit v5 on v4

--- a/solution.py
+++ b/solution.py
@@ -235,8 +235,7 @@
         valid = causal & ((position & (REQS - 1)) == b)
         new_scores[rows, :] = jnp.where(valid, fresh[rows] * SCALE, LOW)
 
-    def attend_group(g):
-        members = range(g * GROUP, (g + 1) * GROUP)
+    def attend_group(members):
         rows = [slice(b * ROWS, (b + 1) * ROWS) for b in members]
         stored = [
             cache[b * TILES : (b + 1) * TILES].reshape(CACHE, 2 * HEAD_DIM) for b in members
@@ -293,7 +292,7 @@
             for load in weight_loads:
                 load.start()
             landing_load.start()
-        attend_group(g)
+        attend_group(range(g * GROUP, (g + 1) * GROUP))
     for g in range(1, GROUPS):
         cache_loads[g].wait()
 
@@ -362,8 +361,8 @@
     for t in range(BATCHES):
         scatter(t)
 
-    for g in range(1, GROUPS):
-        attend_group(g)
+    for b in range(GROUP, REQS, 6):
+        attend_group(range(b, b + 6))
 
     context = acc[...] + jnp.dot(
         new_scores[...].astype(BF16), newest[:, HEAD_DIM:], preferred_element_type=F32

time: 27.2 us -> 27.1 us (level)
  no operation moved by 1% of the time
where the time goes in v5:
time: 27.1 us
  Pallas kernels  26.4 us (97%)
  between operations  0.64 us (2%)
    pallas_call x1, Pallas kernels, on_device(): pl.pallas_call(main_kernel, out_shape=(jax.ShapeDtypeStruct((TOKENS, NARR...  25.6 us
    pallas_call x1, Pallas kernels, on_device(): pl.pallas_call(publish, out_shape=(jax.ShapeDtypeStruct(attended.shape, B...  0.85 us

profile of v5, /device:TPU:1, one launch (start us, length us, event | category | flops | bytes accessed | tf_op | source)
XLA Modules:
  0.0 27.1 jit_solution(5923173211995485192)
XLA Ops:
  0.6 25.6 %shard_map.113 = (bf16[48,512]{1,0:T(8,128)(2,1)S(1)}, bf16[4,256,256]{2,1,0:T(8,128)(2,1)S(1)}) custom-call(s32[16]{0:T(128)} %lengths_hbm.1, s32[1,4]{1,0:T(1,128)} %moving_hbm.1, s32[1,4]{1,0:T(1,128)} %copied_hbm.1, bf16[3,16,1024]{2,1,0:T(8,128)(2,1)} %queries_hbm.1, bf16[48,256]{1,0:T(8,128)(2,1)} %bitcast.9, bf16[1024,16,256]{2,1,0:T(8,128)(2,1)} %bitcast.7, ...), custom_call_target="tpu_custom_call" | custom-call | tf_op jit(solution)/shard_map/pallas_call | solution.py:533
  26.2 0.8 %shard_map.114 = (bf16[48,512]{1,0:T(8,128)(2,1)}, bf16[4,256,256]{2,1,0:T(8,128)(2,1)}) custom-call(bf16[48,512]{1,0:T(8,128)(2,1)S(1)} %get-tuple-element.6.attended, bf16[4,256,256]{2,1,0:T(8,128)(2,1)S(1)} %get-tuple-element.7.landed), custom_call_target="tpu_custom_call" | custom-call | tf_op jit(solution)/shard_map/pallas_call | solution.py:611
